TPU v7x, 32 devices: a whole 2x2x4 slice. The times are simulated.
32 devices in a mesh: dom: 8 (over z, x), band: 4 (over y, core).
Axes of the slice: x: 2, y: 2, z: 4, core: 2. Of those that a mesh axis runs over, the one named last changes fastest.
Arguments:
- orbitals_now: bfloat16 [128, 512, 512], P('dom', 'band'), may hold values from -6 to 6
- orbitals_prev: bfloat16 [128, 512, 512], P('dom', 'band'), may hold values from -6 to 6
- interp: bfloat16 [8, 512, 512], replicated, may hold values from -0.25 to 0.25
- owner_map: int32 [128], replicated, may hold values from 0 to 7, as said below
- child_oct: int32 [128, 2], replicated, may hold values from 0 to 7, all different within a row
Outputs:
- predicted: bfloat16 [512, 512, 512], P(('dom', 'band'))
Inputs may be any that keep to these rules, and one draw needn't show every extreme that they name: `owner_map`: among the 16 cells of one domain at most 4 have the same owner; in every draw one owner receives exactly 4 cells from every domain.
All inputs are finite; a program needn't handle non-finite values.
Results may differ from a plain program's by a relative error of at most 0.0059.
Values may be sent and summed in bfloat16 or wider, within the bound.
A program may use at most 128 MiB of HBM per device.

v0:
```python
import math

import jax
import jax.numpy as jnp
from jax import lax
from jax.sharding import PartitionSpec as P


def refine(parents, octants, interp):
    total_rows, width, node_count = parents.shape
    group_size = math.gcd(total_rows, 4)

    def refine_group(inputs):
        group_cells, picked = inputs
        matrices = jnp.take(interp, picked.reshape(-1), axis=0).reshape(
            group_size, 2, node_count, node_count
        )
        refined = jnp.einsum(
            "psn,pjmn->pjsm", group_cells, matrices, preferred_element_type=jnp.float32
        )
        return refined.astype(jnp.bfloat16)

    grouped = parents.reshape(total_rows // group_size, group_size, width, node_count)
    picked_all = octants.reshape(total_rows // group_size, group_size, 2)
    result = lax.map(refine_group, (grouped, picked_all))
    return result.reshape(total_rows, 2, width, node_count)


def slot_octants(owners, cell_ranks, octants, my_dom, capacity):
    owned_mask = owners == my_dom
    slot_match = owned_mask[:, :, None] & (
        cell_ranks[:, :, None] == jnp.arange(capacity, dtype=jnp.int32)[None, None, :]
    )
    slot_oct = jnp.sum(slot_match.astype(jnp.int32)[:, :, :, None] * octants[:, :, None, :], axis=1)
    return slot_oct.reshape(-1, 2)


def per_device(orbitals_now, orbitals_prev, interp, owner_map, child_oct):
    dom_size = lax.axis_size("dom")
    my_dom = lax.axis_index("dom")
    old_dev, state_dev, node_count = orbitals_now.shape
    capacity = 2 * old_dev // dom_size
    owners = owner_map.reshape(dom_size, old_dev)
    octants = child_oct.reshape(dom_size, old_dev, 2)
    matching = owners[:, :, None] == owners[:, None, :]
    earlier = lax.broadcasted_iota(jnp.int32, (old_dev, old_dev), 1) < lax.broadcasted_iota(
        jnp.int32, (old_dev, old_dev), 0
    )
    cell_ranks = jnp.sum((matching & earlier[None]).astype(jnp.int32), axis=2)
    mine_owner = lax.dynamic_index_in_dim(owners, my_dom, 0, keepdims=False)
    mine_rank = lax.dynamic_index_in_dim(cell_ranks, my_dom, 0, keepdims=False)
    slot_index = mine_owner * capacity + mine_rank
    placing = (
        lax.broadcasted_iota(jnp.int32, (dom_size * capacity, old_dev), 0) == slot_index[None, :]
    ).astype(jnp.bfloat16)
    stacked = jnp.concatenate([orbitals_now, orbitals_prev], axis=1)
    outgoing = jnp.dot(placing, stacked.reshape(old_dev, -1), preferred_element_type=jnp.float32)
    outgoing = outgoing.astype(jnp.bfloat16).reshape(dom_size * capacity, 2 * state_dev, node_count)
    received = lax.all_to_all(outgoing, "dom", split_axis=0, concat_axis=0, tiled=True)
    send_now = received[:, :state_dev]
    send_prev = received[:, state_dev:]
    rows_now, rows_prev = (
        lax.all_to_all(send_now, "band", split_axis=0, concat_axis=1, tiled=True),
        lax.all_to_all(send_prev, "band", split_axis=0, concat_axis=1, tiled=True),
    )
    states = rows_now.shape[1]
    band_size = lax.axis_size("band")
    my_band = lax.axis_index("band")
    slot_count = dom_size * capacity // band_size
    slot_oct = slot_octants(owners, cell_ranks, octants, my_dom, capacity)
    local_oct = lax.dynamic_slice_in_dim(slot_oct, my_band * slot_count, slot_count, 0)
    whole_parents = jnp.concatenate([rows_now, rows_prev], axis=1)
    refined_rows = refine(whole_parents, local_oct, interp)
    rows_now = refined_rows[:, :, :states].reshape(-1, states, node_count)
    rows_prev = refined_rows[:, :, states:].reshape(-1, states, node_count)
    partial_value = jnp.einsum(
        "csm,ctm->st", rows_now, rows_prev, preferred_element_type=jnp.float32
    )
    scaling = 1.0 / math.sqrt(2.0 * states * owner_map.shape[0] * node_count)
    intersection = lax.psum(partial_value, ("dom", "band")) * scaling
    intersection_b = intersection.astype(jnp.bfloat16)
    mixed = jnp.einsum("st,csm->ctm", intersection_b, rows_now, preferred_element_type=jnp.float32)
    return (rows_prev.astype(jnp.float32) + mixed).astype(jnp.bfloat16)


def solution(mesh):
    in_specs = (P("dom", "band", None), P("dom", "band", None), P(), P(), P())
    out_specs = P(("dom", "band"), None, None)
    return jax.shard_map(
        per_device, mesh=mesh, in_specs=in_specs, out_specs=out_specs, check_vma=False
    )
```

profile of v0, /device:TPU:19, one launch (start us, length us, event | category | flops | bytes accessed | tf_op | source)
XLA Modules:
  0.0 593.7 jit_solution(14590287565571533165)
XLA Ops:
  14.5 7.9 %convolution_convert_fusion = bf16[32,131072]{1,0:T(8,128)(2,1)} fusion(bf16[16,131072]{1,0:T(8,128)(2,1)} %bitcast.69, s32[16]{0:T(128)S(1)} %fusion.17), kind=kOutput, calls=%fused_computation.16 | convolution fusion | flops 138412544 | bytes 12582976 | tf_op jit(solution)/shard_map/dot_general | solution.py:57
  22.4 9.8 %copy.37 = bf16[4,8,256,512]{3,2,1,0:T(8,128)(2,1)} copy(bf16[4,8,256,512]{3,1,2,0:T(8,128)(2,1)} %bitcast.63) | data formatting | bytes 16777216
  32.2 185.2 %all_to_all.35 = bf16[32,256,512]{2,1,0:T(8,128)(2,1)S(1)} all-to-all(bf16[32,256,512]{2,1,0:T(8,128)(2,1)} %bitcast.64), channel_id=1, replica_groups=mesh['dom'=8,'band'=4] {'dom'}, dimensions={0} | all-to-all | bytes 16777216 | tf_op jit(solution)/shard_map/all_to_all | solution.py:59
  219.7 52.0 %all_to_all.36 = bf16[32,128,512]{2,1,0:T(8,128)(2,1)} all-to-all(bf16[32,128,512]{2,1,0:T(8,128)(2,1)S(1)} %get-tuple-element.60), channel_id=1, replica_groups=mesh['dom'=8,'band'=4] {'band'}, dimensions={0} | all-to-all | bytes 8388608 | tf_op jit(solution)/shard_map/all_to_all | solution.py:63
  271.7 5.9 all-to-all-start.2
  278.3 4.6 copy.23
  282.9 42.1 %all-to-all-done.2 = bf16[32,128,512]{2,1,0:T(8,128)(2,1)} async-done(((bf16[32,128,512]{2,1,0:T(8,128)(2,1)}), bf16[32,128,512]{2,1,0:T(8,128)(2,1)}, u32[]{:S(2)}, u32[]{:S(2)}) %all-to-all-start.2) | async-done | bytes 4194336 | tf_op jit(solution)/shard_map/all_to_all | solution.py:64
  329.6 7.4 %pad_maximum_fusion = bf16[2,4,1024,512]{3,2,1,0:T(8,128)(2,1)} fusion(bf16[2,4,512,512]{3,2,1,0:T(8,128)(2,1)} %bitcast.72, bf16[2,4,512,512]{3,2,1,0:T(8,128)(2,1)} %bitcast.71), kind=kLoop, calls=%fused_computation.19 | loop fusion | flops 16777216 | bytes 16777216 | tf_op jit(solution)/shard_map/concatenate | solution.py:72
  337.0 70.0 %while.10 = (s32[]{:T(128)}, bf16[2,4,2,1024,512]{4,3,2,1,0:T(8,128)(2,1)}, s32[2,4,2]{2,1,0:T(4,128)S(1)}, bf16[8,512,512]{2,1,0:T(8,128)(2,1)}, bf16[2,4,1024,512]{3,2,1,0:T(8,128)(2,1)}, /*index=5*/s32[]{:T(128)}) while((s32[]{:T(128)}, bf16[2,4,2,1024,512]{4,3,2,1,0:T(8,128)(2,1)}, s32[2,4,2]{2,1,0:T(4,128)S(1)}, ...), condition=%wide.region_3.4_spmd, body=%wide.region_2.3_spmd.sunk | while | flops 4301259776 | bytes 58724824 | solution.py:25
  337.3 4.9 gather_fusion
  342.3 11.2 %convert_bitcast_fusion.2 = bf16[1,4,2,1024,512]{3,4,2,1,0:T(8,128)(2,1)} fusion(bf16[2,4,1024,512]{3,2,1,0:T(8,128)(2,1)} %get-tuple-element.109, s32[]{:T(128)S(6)} %copy.47, bf16[4,2,512,512]{3,2,1,0:T(8,128)(2,1)} %bitcast.62, pred[4,2]{1,0:T(4,128)(4,1)S(1)} %copy.42), kind=kOutput, calls=%fused_computation.1.clone.1 | convolution fusion | flops 4301258752 | bytes 16777228 | tf_op jit(solution)/shard_map/while/body/eval_jaxpr/psn,pjmn->pjsm/dot_general | solution.py:18
  353.5 11.4 %copy.43 = bf16[1,4,2,1024,512]{4,3,2,1,0:T(8,128)(2,1)} copy(bf16[1,4,2,1024,512]{3,4,2,1,0:T(8,128)(2,1)} %convert_bitcast_fusion.2) | data formatting | bytes 16777216 | tf_op jit(solution)/shard_map/while/body/jit(dynamic_update_index_in_dim)/dynamic_update_slice | solution.py:25
  364.9 7.1 %constant_dynamic-update-slice_fusion.2 = bf16[2,4,2,1024,512]{4,3,2,1,0:T(8,128)(2,1)} fusion(bf16[2,4,2,1024,512]{4,3,2,1,0:T(8,128)(2,1)} %get-tuple-element.100, bf16[1,4,2,1024,512]{4,3,2,1,0:T(8,128)(2,1)} %copy.43, s32[]{:T(128)S(6)} %copy.47), kind=kLoop, calls=%fused_computation.11.clone.1 | loop fusion | bytes 16777220 | tf_op jit(solution)/shard_map/while/body/jit(dynamic_update_index_in_dim)/dynamic_update_slice | solution.py:25
  372.3 4.9 gather_fusion
  377.3 11.2 %convert_bitcast_fusion.2 = bf16[1,4,2,1024,512]{3,4,2,1,0:T(8,128)(2,1)} fusion(bf16[2,4,1024,512]{3,2,1,0:T(8,128)(2,1)} %get-tuple-element.109, s32[]{:T(128)S(6)} %copy.47, bf16[4,2,512,512]{3,2,1,0:T(8,128)(2,1)} %bitcast.62, pred[4,2]{1,0:T(4,128)(4,1)S(1)} %copy.42), kind=kOutput, calls=%fused_computation.1.clone.1 | convolution fusion | flops 4301258752 | bytes 16777228 | tf_op jit(solution)/shard_map/while/body/eval_jaxpr/psn,pjmn->pjsm/dot_general | solution.py:18
  388.5 11.4 %copy.43 = bf16[1,4,2,1024,512]{4,3,2,1,0:T(8,128)(2,1)} copy(bf16[1,4,2,1024,512]{3,4,2,1,0:T(8,128)(2,1)} %convert_bitcast_fusion.2) | data formatting | bytes 16777216 | tf_op jit(solution)/shard_map/while/body/jit(dynamic_update_index_in_dim)/dynamic_update_slice | solution.py:25
  399.9 7.1 %constant_dynamic-update-slice_fusion.2 = bf16[2,4,2,1024,512]{4,3,2,1,0:T(8,128)(2,1)} fusion(bf16[2,4,2,1024,512]{4,3,2,1,0:T(8,128)(2,1)} %get-tuple-element.100, bf16[1,4,2,1024,512]{4,3,2,1,0:T(8,128)(2,1)} %copy.43, s32[]{:T(128)S(6)} %copy.47), kind=kLoop, calls=%fused_computation.11.clone.1 | loop fusion | bytes 16777220 | tf_op jit(solution)/shard_map/while/body/jit(dynamic_update_index_in_dim)/dynamic_update_slice | solution.py:25
  407.0 11.3 %convolution_bitcast_fusion = f32[512,512]{1,0:T(8,128)} fusion(bf16[8,2,1024,512]{3,2,1,0:T(8,128)(2,1)} %bitcast.66), kind=kOutput, calls=%fused_computation.22 | convolution fusion | flops 4294967296 | bytes 17825792 | tf_op jit(solution)/shard_map/csm,ctm->st/dot_general | solution.py:76
  418.3 11.4 %fusion.21 = (bf16[8,2,512,512]{3,2,1,0:T(8,128)(2,1)}, bf16[8,2,512,512]{3,2,1,0:T(8,128)(2,1)}) fusion(bf16[8,2,1024,512]{3,2,1,0:T(8,128)(2,1)} %bitcast.67), kind=kLoop, calls=%fused_computation.44 | loop fusion | bytes 33554432 | tf_op jit(solution)/shard_map/slice | solution.py:74
  429.8 11.5 %bitcast_convert_fusion = f32[16,512,512]{2,1,0:T(8,128)} fusion(bf16[8,2,512,512]{3,2,1,0:T(8,128)(2,1)} %get-tuple-element.59), kind=kLoop, calls=%fused_computation.20 | loop fusion | flops 4194304 | bytes 25165824 | tf_op jit(solution)/shard_map/convert_element_type | solution.py:83
  441.2 17.7 %copy.28 = f32[16,512,512]{1,2,0:T(8,128)} copy(f32[16,512,512]{2,1,0:T(8,128)} %bitcast_convert_fusion) | data formatting | bytes 33554432 | tf_op jit(solution)/shard_map/convert_element_type | solution.py:83
  458.9 99.5 %all-reduce.2.cloned.1.call-done = f32[512,512]{1,0:T(8,128)} async-done(((f32[512,512]{1,0:T(8,128)}), f32[512,512]{1,0:T(8,128)}) %all-reduce.2.cloned.1.call-update) | async-done | bytes 1048592 | tf_op jit(solution)/shard_map/psum | solution.py:80
  558.4 16.3 %fusion.8 = bf16[16,512,512]{1,2,0:T(8,128)(2,1)} fusion(f32[16,512,512]{1,2,0:T(8,128)} %copy.28, bf16[16,512,512]{2,1,0:T(8,128)(2,1)} %bitcast.65, f32[512,512]{1,0:T(8,128)} %all-reduce.2.cloned.1.call-done), kind=kOutput, calls=%fused_computation.18 | convolution fusion | flops 4303880192 | bytes 34603008 | tf_op jit(solution)/shard_map/st,csm->ctm/dot_general | solution.py:82
  574.6 12.3 %copy.29 = bf16[16,512,512]{2,1,0:T(8,128)(2,1)} copy(bf16[16,512,512]{1,2,0:T(8,128)(2,1)} %fusion.8) | data formatting | bytes 16777216 | tf_op jit(solution)/shard_map/convert_element_type | solution.py:83
  (35 shorter events, 16.1 us)
Async XLA Ops:
  219.7 57.9 %copy-start = (s32[128,2]{0,1:T(2,128)S(1)}, s32[128,2]{0,1:T(2,128)}, u32[]{:S(2)}) copy-start(s32[128,2]{0,1:T(2,128)} %param.11) | copy-start | bytes 3076
  271.7 53.3 %all-to-all-start.2 = ((bf16[32,128,512]{2,1,0:T(8,128)(2,1)}), bf16[32,128,512]{2,1,0:T(8,128)(2,1)}, u32[]{:S(2)}, u32[]{:S(2)}) async-start(bf16[32,128,512]{2,1,0:T(8,128)(2,1)} %get-tuple-element.61), calls=%async_computation.2 | async-start | bytes 8388608 | tf_op jit(solution)/shard_map/all_to_all | solution.py:64
  277.6 280.8 %all-reduce.2.cloned.1.call-start = ((), (), s32[]{:S(2)}) async-start(), calls=%async_computation.3 | async-start | bytes 2097152 | tf_op jit(solution)/shard_map/psum | solution.py:80
Sparse Core Ops, SparseCore 0:
  429.9 128.4 all-reduce.1
where the time goes:
time: 600 us; the launch traced here: 594 us
  blocking collectives  237 us (40%)
  waiting for transfers between devices  142 us (24%)
  local copies, waits for them, and re-layouts  116 us (19%)
  matrix products  57.9 us (10%)
  other arithmetic  22 us (4%)
  between operations  13.4 us (2%)
    all_to_all x1, blocking collectives, per_device(): lax.all_to_all(outgoing, 'dom', split_axis=0, concat_axis=0, tiled=True)  185 us
    psum x1, waiting for transfers between devices, per_device(): intersection = lax.psum(partial_value, ('dom', 'band')) * scaling  99.5 us
    all_to_all x1, blocking collectives, per_device(): lax.all_to_all(send_now, 'band', split_axis=0, concat_axis=1, tiled=True)  52 us
    all_to_all x1, waiting for transfers between devices, per_device(): lax.all_to_all(send_prev, 'band', split_axis=0, concat_axis=1, tiled=True)  42.1 us
    dynamic_update_slice x4, local copies, waits for them, and re-layouts, refine(): result = lax.map(refine_group, (grouped, picked_all))  37.1 us
    convert_element_type x2, local copies, waits for them, and re-layouts, per_device(): return (rows_prev.astype(jnp.float32) + mixed).astype(jnp.bfloat16)  29.9 us
    dot_general x2, matrix products, refine_group(): jnp.einsum('psn,pjmn->pjsm', group_cells, matrices, preferred_element_typ...  22.4 us
    dot_general x1, matrix products, per_device(): jnp.einsum('st,csm->ctm', intersection_b, rows_now, preferred_element_typ...  16.3 us
  transfers between devices with their start and end apart: 2, of which 2 were waited for; matrix products, arithmetic and copies ran while one was open for 6% of the time, Pallas kernels for 0%

commit v1 on v0

v1 whole, which is shorter than its diff:
```python
import functools
import math

import jax
import jax.numpy as jnp
from jax import lax
from jax.experimental import pallas as pl
from jax.experimental.pallas import tpu as pltpu
from jax.sharding import PartitionSpec as P

NT = (((1,), (1,)), ((), ()))
TN = (((0,), (0,)), ((), ()))


def mm(a, b, dims=(((1,), (0,)), ((), ()))):
    return lax.dot_general(a, b, dims, preferred_element_type=jnp.float32)


def gather_band(block):
    band_size = lax.axis_size("band")
    have = {0: block}
    bit = band_size // 2
    while bit:
        perm = [(b, b ^ bit) for b in range(band_size)]
        for off in list(have):
            have[off ^ bit] = lax.ppermute(have[off], "band", perm)
        bit //= 2
    return [have[off] for off in range(band_size)]


def fold_kernel(oct_ref, prev_ref, first_ref, second_ref, out_ref):
    prev = prev_ref[0]
    total = None
    for interp_ref in (first_ref, second_ref):
        child = mm(prev, interp_ref[0], NT).astype(jnp.bfloat16)
        back = mm(child, interp_ref[0])
        total = back if total is None else total + back
    out_ref[0] = total.astype(jnp.bfloat16)


def fold(prev, interp, octants):
    cells, width, nodes = prev.shape
    return pl.pallas_call(
        fold_kernel,
        out_shape=jax.ShapeDtypeStruct(prev.shape, jnp.bfloat16),
        grid_spec=pltpu.PrefetchScalarGridSpec(
            num_scalar_prefetch=1,
            grid=(cells,),
            in_specs=[
                pl.BlockSpec((1, width, nodes), lambda g, o: (g, 0, 0)),
                pl.BlockSpec((1, nodes, nodes), lambda g, o: (o[2 * g], 0, 0)),
                pl.BlockSpec((1, nodes, nodes), lambda g, o: (o[2 * g + 1], 0, 0)),
            ],
            out_specs=pl.BlockSpec((1, width, nodes), lambda g, o: (g, 0, 0)),
        ),
        compiler_params=pltpu.CompilerParams(vmem_limit_bytes=32 * 2**20),
        cost_estimate=pl.CostEstimate(
            flops=8 * cells * width * nodes * nodes,
            bytes_accessed=4 * cells * nodes * (width + nodes),
            transcendentals=0,
        ),
        name="fold",
    )(octants.reshape(-1), prev, interp, interp)


def overlap_kernel(count, *refs):
    now_refs, folded_ref, out_ref = refs[:count], refs[count], refs[count + 1]

    @pl.when(pl.program_id(0) == 0)
    def _():
        out_ref[...] = jnp.zeros_like(out_ref)

    for k in range(count):
        out_ref[k] += mm(now_refs[k][0], folded_ref[0], NT)


def overlap(nows, folded):
    cells, width, nodes = folded.shape
    count = len(nows)
    block = pl.BlockSpec((1, width, nodes), lambda g: (g, 0, 0))
    return pl.pallas_call(
        functools.partial(overlap_kernel, count),
        out_shape=jax.ShapeDtypeStruct((count, width, width), jnp.float32),
        grid=(cells,),
        in_specs=[block] * (count + 1),
        out_specs=pl.BlockSpec((count, width, width), lambda g: (0, 0, 0)),
        compiler_params=pltpu.CompilerParams(vmem_limit_bytes=32 * 2**20),
        name="overlap",
    )(*nows, folded)


def correct_kernel(count, slot_ref, *refs):
    now_refs, prev_ref, mix_ref, out_ref = refs[:count], refs[count], refs[count + 1], refs[count + 2]
    total = prev_ref[0].astype(jnp.float32)
    for k in range(count):
        total = total + mm(mix_ref[k], now_refs[k][0], TN)
    out_ref[0] = total.astype(jnp.bfloat16)


def correct(nows, prev, mix, slot_index, slots):
    cells, width, nodes = prev.shape
    count = len(nows)
    block = pl.BlockSpec((1, width, nodes), lambda g, s: (g, 0, 0))
    return pl.pallas_call(
        functools.partial(correct_kernel, count),
        out_shape=jax.ShapeDtypeStruct((slots, width, nodes), jnp.bfloat16),
        grid_spec=pltpu.PrefetchScalarGridSpec(
            num_scalar_prefetch=1,
            grid=(cells,),
            in_specs=[block] * (count + 1)
            + [pl.BlockSpec((count, width, width), lambda g, s: (0, 0, 0))],
            out_specs=pl.BlockSpec((1, width, nodes), lambda g, s: (s[g], 0, 0)),
        ),
        compiler_params=pltpu.CompilerParams(vmem_limit_bytes=32 * 2**20),
        name="correct",
    )(slot_index, *nows, prev, mix)


def expand_kernel(valid_ref, oct_ref, rows_ref, interp_ref, out_ref):
    band, _, width, nodes = rows_ref.shape
    valid = valid_ref[pl.program_id(0)] > 0

    @pl.when(valid)
    def _():
        for b in range(band):
            out_ref[0, b * width : (b + 1) * width] = mm(
                rows_ref[b, 0], interp_ref[0], NT
            ).astype(jnp.bfloat16)

    @pl.when(jnp.logical_not(valid))
    def _():
        out_ref[...] = jnp.zeros_like(out_ref)


def expand(rows, interp, valid, octants):
    band, slots, width, nodes = rows.shape
    return pl.pallas_call(
        expand_kernel,
        out_shape=jax.ShapeDtypeStruct((2 * slots, band * width, nodes), jnp.bfloat16),
        grid_spec=pltpu.PrefetchScalarGridSpec(
            num_scalar_prefetch=2,
            grid=(slots, 2),
            in_specs=[
                pl.BlockSpec((band, 1, width, nodes), lambda s, j, v, o: (0, s, 0, 0)),
                pl.BlockSpec((1, nodes, nodes), lambda s, j, v, o: (o[2 * s + j], 0, 0)),
            ],
            out_specs=pl.BlockSpec((1, band * width, nodes), lambda s, j, v, o: (2 * s + j, 0, 0)),
        ),
        compiler_params=pltpu.CompilerParams(vmem_limit_bytes=32 * 2**20),
        name="expand",
    )(valid, octants.reshape(-1), rows, interp)


def per_device(orbitals_now, orbitals_prev, interp, owner_map, child_oct):
    dom_size = lax.axis_size("dom")
    band_size = lax.axis_size("band")
    my_dom = lax.axis_index("dom")
    my_band = lax.axis_index("band")
    old_dev, state_dev, node_count = orbitals_now.shape
    states = state_dev * band_size
    capacity = 2 * old_dev // dom_size
    owners = owner_map.reshape(dom_size, old_dev)
    octants = child_oct.reshape(dom_size, old_dev, 2)
    matching = owners[:, :, None] == owners[:, None, :]
    earlier = lax.broadcasted_iota(jnp.int32, (old_dev, old_dev), 1) < lax.broadcasted_iota(
        jnp.int32, (old_dev, old_dev), 0
    )
    ranks = jnp.sum((matching & earlier[None]).astype(jnp.int32), axis=2)
    slot_all = owners * capacity + ranks
    slot_index = lax.dynamic_index_in_dim(slot_all, my_dom, 0, keepdims=False)
    my_octants = lax.dynamic_index_in_dim(octants, my_dom, 0, keepdims=False)
    slot_count = dom_size * capacity // band_size
    source_count = slot_count // capacity
    near = lax.dynamic_slice_in_dim(slot_all, my_band * source_count, source_count, 0)
    near_oct = lax.dynamic_slice_in_dim(octants, my_band * source_count, source_count, 0)
    wanted = my_dom * capacity + jnp.arange(capacity, dtype=jnp.int32)
    hit = (near[:, None, :] == wanted[None, :, None]).astype(jnp.int32)
    valid = jnp.sum(hit, axis=2).reshape(-1)
    slot_oct = jnp.sum(hit[..., None] * near_oct[:, None], axis=2).reshape(-1, 2)

    nows = gather_band(orbitals_now)
    folded = fold(orbitals_prev, interp, my_octants)
    partial = overlap(nows, folded)
    scaling = 1.0 / math.sqrt(2.0 * states * owner_map.shape[0] * node_count)
    mix = (lax.psum(partial, "dom") * scaling).astype(jnp.bfloat16)
    outgoing = correct(nows, orbitals_prev, mix, slot_index, dom_size * capacity)
    received = lax.all_to_all(outgoing, "dom", split_axis=0, concat_axis=0, tiled=True)
    rows = lax.all_to_all(received, "band", split_axis=0, concat_axis=0, tiled=True)
    rows = rows.reshape(band_size, slot_count, state_dev, node_count)
    return expand(rows, interp, valid, slot_oct)


def solution(mesh):
    in_specs = (P("dom", "band", None), P("dom", "band", None), P(), P(), P())
    out_specs = P(("dom", "band"), None, None)
    return jax.shard_map(
        per_device, mesh=mesh, in_specs=in_specs, out_specs=out_specs, check_vma=False
    )
```

time: 600 us -> 346 us (0.58)
  blocking collectives: 237 us -> 93.3 us
  local copies, waits for them, and re-layouts: 116 us -> 9.53 us
  matrix products: 57.9 us -> 0 us
  Pallas kernels: 0 us -> 51.6 us
  other arithmetic: 22 us -> 1.67 us
  waiting for transfers between devices: 142 us -> 160 us
    all_to_all x1, blocking collectives: 185 us -> 93.3 us  [per_device(): lax.all_to_all(outgoing, 'dom', split_axis=0, concat_axis=0, tiled=True)]
    dot_general x5 -> x0, matrix products: 57.9 us -> none  [the longest x2 22.4 us: refine_group(): jnp.einsum('psn,pjmn->pjsm', group_cells, matrices, preferred_element_typ...]
    all_to_all x1 -> x0, blocking collectives: 52 us -> none  [per_device(): lax.all_to_all(send_now, 'band', split_axis=0, concat_axis=1, tiled=True)]
    pallas_call x0 -> x4, Pallas kernels: none -> 51.6 us  [the longest x1 15.6 us: expand(): pl.pallas_call(expand_kernel, out_shape=jax.ShapeDtypeStruct((2 * slots,...]
    ppermute x0 -> x3, waiting for transfers between devices: none -> 44.6 us  [gather_band(): have[off ^ bit] = lax.ppermute(have[off], 'band', perm)]
    dynamic_update_slice x4 -> x0, local copies, waits for them, and re-layouts: 37.1 us -> none  [refine(): result = lax.map(refine_group, (grouped, picked_all))]
    psum x1, waiting for transfers between devices: 99.5 us -> 68.5 us  [per_device(): mix = (lax.psum(partial, 'dom') * scaling).astype(jnp.bfloat16)]
    convert_element_type x2 -> x0, local copies, waits for them, and re-layouts: 29.9 us -> none  [per_device(): return (rows_prev.astype(jnp.float32) + mixed).astype(jnp.bfloat16)]
  transfers between devices with their start and end apart: 2 -> 5, of which waited for: 2 -> 3; matrix products, arithmetic and copies ran while one was open for 6% -> 1% of each run, Pallas kernels for 0% -> 4%
where the time goes in v1:
time: 346 us; the launch traced here: 340 us
  waiting for transfers between devices  160 us (46%)
  blocking collectives  93.3 us (27%)
  Pallas kernels  51.6 us (15%)
  between operations  13.5 us (4%)
  starting transfers between devices  11 us (3%)
  local copies, waits for them, and re-layouts  9.53 us (3%)
    all_to_all x1, blocking collectives, per_device(): lax.all_to_all(outgoing, 'dom', split_axis=0, concat_axis=0, tiled=True)  93.3 us
    psum x1, waiting for transfers between devices, per_device(): mix = (lax.psum(partial, 'dom') * scaling).astype(jnp.bfloat16)  68.5 us
    all_to_all x1, waiting for transfers between devices, per_device(): lax.all_to_all(received, 'band', split_axis=0, concat_axis=0, tiled=True)  46.7 us
    ppermute x3, waiting for transfers between devices, gather_band(): have[off ^ bit] = lax.ppermute(have[off], 'band', perm)  44.6 us
    pallas_call x1, Pallas kernels, expand(): pl.pallas_call(expand_kernel, out_shape=jax.ShapeDtypeStruct((2 * slots,...  15.6 us
    pallas_call x1, Pallas kernels, fold(): pl.pallas_call(fold_kernel, out_shape=jax.ShapeDtypeStruct(prev.shape, jn...  12.2 us
    pallas_call x1, Pallas kernels, overlap(): pl.pallas_call(functools.partial(overlap_kernel, count), out_shape=jax.Sh...  11.9 us
    pallas_call x1, Pallas kernels, correct(): pl.pallas_call(functools.partial(correct_kernel, count), out_shape=jax.Sh...  11.9 us
  transfers between devices with their start and end apart: 5, of which 3 were waited for; matrix products, arithmetic and copies ran while one was open for 1% of the time, Pallas kernels for 4%

profile of v1, /device:TPU:19, one launch (start us, length us, event | category | flops | bytes accessed | tf_op | source)
XLA Modules:
  0.0 340.4 jit_solution(11644338081741742561)
XLA Ops:
  6.5 1.2 collective-permute-start.1
  7.8 1.0 collective-permute-start
  8.7 44.6 %collective-permute-done.1.refs_2_ = bf16[16,128,512]{2,1,0:T(8,128)(2,1)} collective-permute-done((bf16[16,128,512]{2,1,0:T(8,128)(2,1)}, bf16[16,128,512]{2,1,0:T(8,128)(2,1)}, u32[]{:S(2)}, u32[]{:S(2)}) %collective-permute-start.1) | collective-permute-done | bytes 2097184 | tf_op jit(solution)/shard_map/ppermute | solution.py:26
  53.4 1.5 collective-permute-start.2
  54.9 0.7 reshape.33
  55.6 0.8 reshape.35
  56.5 0.1 reshape.36.oct_ref
  56.6 0.3 convert_reduce_fusion
  56.9 2.2 copy-done.1
  59.1 1.6 copy-done.3
  60.7 12.2 %fold.1.refs_4_ = bf16[16,128,512]{2,1,0:T(8,128)(2,1)S(1)} custom-call(s32[32]{0:T(128)S(1)} %reshape.36.oct_ref, bf16[16,128,512]{2,1,0:T(8,128)(2,1)S(1)} %copy-done.3, bf16[8,512,512]{2,1,0:T(8,128)(2,1)S(1)} %copy-done.1, bf16[8,512,512]{2,1,0:T(8,128)(2,1)S(1)} %copy-done.1), custom_call_target="tpu_custom_call" | custom-call | flops 4294967296 | bytes 20971520 | tf_op jit(solution)/shard_map/fold/pallas_call | solution.py:43
  72.9 11.9 %overlap.1 = f32[4,128,128]{2,1,0:T(8,128)} custom-call(bf16[16,128,512]{2,1,0:T(8,128)(2,1)S(1)} %copy-done, bf16[16,128,512]{2,1,0:T(8,128)(2,1)} %collective-permute-done.refs_1_, bf16[16,128,512]{2,1,0:T(8,128)(2,1)} %collective-permute-done.1.refs_2_, bf16[16,128,512]{2,1,0:T(8,128)(2,1)} %collective-permute-done.2.refs_3_, ...), custom_call_target="tpu_custom_call" | custom-call | tf_op jit(solution)/shard_map/overlap/pallas_call | solution.py:81
  84.8 68.5 %all-reduce.2.cloned.1.call-done = f32[4,128,128]{2,1,0:T(8,128)} async-done(((f32[4,128,128]{2,1,0:T(8,128)}), f32[4,128,128]{2,1,0:T(8,128)}) %all-reduce.2.cloned.1.call-update) | async-done | bytes 262160 | tf_op jit(solution)/shard_map/psum | solution.py:185
  153.3 1.0 multiply_convert_fusion.refs_5_
  154.3 1.6 copy-done.4
  155.9 11.9 %correct.1 = bf16[32,128,512]{2,1,0:T(8,128)(2,1)S(1)} custom-call(s32[16]{0:T(128)S(1)} %fusion.slot_ref, bf16[16,128,512]{2,1,0:T(8,128)(2,1)S(1)} %copy-done, bf16[16,128,512]{2,1,0:T(8,128)(2,1)} %collective-permute-done.refs_1_, bf16[16,128,512]{2,1,0:T(8,128)(2,1)} %collective-permute-done.1.refs_2_, ...), custom_call_target="tpu_custom_call" | custom-call | tf_op jit(solution)/shard_map/correct/pallas_call | solution.py:104
  167.8 93.3 %all_to_all.10 = bf16[32,128,512]{2,1,0:T(8,128)(2,1)} all-to-all(bf16[32,128,512]{2,1,0:T(8,128)(2,1)S(1)} %correct.1), channel_id=1, replica_groups=mesh['dom'=8,'band'=4] {'dom'}, dimensions={0} | all-to-all | bytes 8388608 | tf_op jit(solution)/shard_map/all_to_all | solution.py:187
  261.1 7.3 %all-to-all-start.1 = ((bf16[32,128,512]{2,1,0:T(8,128)(2,1)}), bf16[32,128,512]{2,1,0:T(8,128)(2,1)}, u32[]{:S(2)}, u32[]{:S(2)}) async-start(bf16[32,128,512]{2,1,0:T(8,128)(2,1)} %all_to_all.10), calls=%async_computation.1 | async-start | bytes 8388608 | tf_op jit(solution)/shard_map/all_to_all | solution.py:188
  268.3 0.2 fusion.1
  268.7 0.1 multiply_reduce_fusion
  268.8 0.1 copy.11
  269.0 46.7 %all-to-all-done.1 = bf16[32,128,512]{2,1,0:T(8,128)(2,1)} async-done(((bf16[32,128,512]{2,1,0:T(8,128)(2,1)}), bf16[32,128,512]{2,1,0:T(8,128)(2,1)}, u32[]{:S(2)}, u32[]{:S(2)}) %all-to-all-start.1) | async-done | bytes 4194336 | tf_op jit(solution)/shard_map/all_to_all | solution.py:188
  315.7 2.2 copy-done.2
  317.9 15.6 %expand.1 = bf16[16,512,512]{2,1,0:T(8,128)(2,1)} custom-call(s32[8]{0:T(128)S(1)} %reshape.34.valid_ref, s32[16]{0:T(128)S(1)} %reshape_reshape.3.oct_ref, bf16[4,8,128,512]{3,2,1,0:T(8,128)(2,1)} %bitcast.1.rows_ref, bf16[8,512,512]{2,1,0:T(8,128)(2,1)S(1)} %copy-done.2), custom_call_target="tpu_custom_call" | custom-call | tf_op jit(solution)/shard_map/expand/pallas_call | solution.py:137
  (22 shorter events, 0.4 us)
Async XLA Ops:
  6.5 146.8 %all-reduce.2.cloned.1.call-start = ((), (), s32[]{:S(2)}) async-start(), calls=%async_computation.2 | async-start | bytes 524288 | tf_op jit(solution)/shard_map/psum | solution.py:185
  6.5 46.8 %collective-permute-start.1 = (bf16[16,128,512]{2,1,0:T(8,128)(2,1)}, bf16[16,128,512]{2,1,0:T(8,128)(2,1)}, u32[]{:S(2)}, u32[]{:S(2)}) collective-permute-start(bf16[16,128,512]{2,1,0:T(8,128)(2,1)} %refs_0_.3), channel_id=1, source_target_pairs={{0,2},{1,3},{2,0},{3,1},{4,6},{5,7},{6,4},{7,5},{8,10},{9,11},{10,... | collective-permute-start | bytes 6291464 | tf_op jit(solution)/shard_map/ppermute | solution.py:26
  7.8 65.1 %collective-permute-start = (bf16[16,128,512]{2,1,0:T(8,128)(2,1)}, bf16[16,128,512]{2,1,0:T(8,128)(2,1)}, u32[]{:S(2)}, u32[]{:S(2)}) collective-permute-start(bf16[16,128,512]{2,1,0:T(8,128)(2,1)} %refs_0_.3), channel_id=1, source_target_pairs={{0,1},{1,0},{2,3},{3,2},{4,5},{5,4},{6,7},{7,6},{8,9},{9,8},{10,11... | collective-permute-start | bytes 6291464 | tf_op jit(solution)/shard_map/ppermute | solution.py:26
  53.4 19.5 %collective-permute-start.2 = (bf16[16,128,512]{2,1,0:T(8,128)(2,1)}, bf16[16,128,512]{2,1,0:T(8,128)(2,1)}, u32[]{:S(2)}, u32[]{:S(2)}) collective-permute-start(bf16[16,128,512]{2,1,0:T(8,128)(2,1)} %collective-permute-done.1.refs_2_), channel_id=1, source_target_pairs={{0,1},{1,0},{2,3},{3,2},{4,5},{5,4},{6,7},{7,6},{8,9},{9,8},{10,11... | collective-permute-start | bytes 6291464 | tf_op jit(solution)/shard_map/ppermute | solution.py:26
  56.9 2.2 copy-start.1
  59.1 1.6 copy-start.3
  60.7 12.2 %copy-start = (bf16[16,128,512]{2,1,0:T(8,128)(2,1)S(1)}, bf16[16,128,512]{2,1,0:T(8,128)(2,1)}, u32[]{:S(2)}) copy-start(bf16[16,128,512]{2,1,0:T(8,128)(2,1)} %refs_0_.3) | copy-start | bytes 6291460
  154.3 1.6 copy-start.4
  261.1 54.7 %all-to-all-start.1 = ((bf16[32,128,512]{2,1,0:T(8,128)(2,1)}), bf16[32,128,512]{2,1,0:T(8,128)(2,1)}, u32[]{:S(2)}, u32[]{:S(2)}) async-start(bf16[32,128,512]{2,1,0:T(8,128)(2,1)} %all_to_all.10), calls=%async_computation.1 | async-start | bytes 8388608 | tf_op jit(solution)/shard_map/all_to_all | solution.py:188
  315.7 2.2 copy-start.2
Sparse Core Ops, SparseCore 0:
  84.9 68.3 all-reduce.1

commit v2 on v1

--- a/solution.py
+++ b/solution.py
@@ -9,14 +9,13 @@
 from jax.sharding import PartitionSpec as P
 
 NT = (((1,), (1,)), ((), ()))
-TN = (((0,), (0,)), ((), ()))
 
 
 def mm(a, b, dims=(((1,), (0,)), ((), ()))):
     return lax.dot_general(a, b, dims, preferred_element_type=jnp.float32)
 
 
-def gather_band(block):
+def gather_band(block, beside):
     band_size = lax.axis_size("band")
     have = {0: block}
     bit = band_size // 2
@@ -24,8 +23,10 @@
         perm = [(b, b ^ bit) for b in range(band_size)]
         for off in list(have):
             have[off ^ bit] = lax.ppermute(have[off], "band", perm)
+        if 2 * bit == band_size:
+            have[bit], beside = lax.optimization_barrier((have[bit], beside))
         bit //= 2
-    return [have[off] for off in range(band_size)]
+    return [have[off] for off in range(band_size)], beside
 
 
 def fold_kernel(oct_ref, prev_ref, first_ref, second_ref, out_ref):
@@ -71,17 +72,21 @@
         out_ref[...] = jnp.zeros_like(out_ref)
 
     for k in range(count):
-        out_ref[k] += mm(now_refs[k][0], folded_ref[0], NT)
+        total = out_ref[k]
+        for at in range(folded_ref.shape[0]):
+            total = total + mm(now_refs[k][at], folded_ref[at], NT)
+        out_ref[k] = total
 
 
 def overlap(nows, folded):
     cells, width, nodes = folded.shape
     count = len(nows)
-    block = pl.BlockSpec((1, width, nodes), lambda g: (g, 0, 0))
+    group = math.gcd(cells, 4)
+    block = pl.BlockSpec((group, width, nodes), lambda g: (g, 0, 0))
     return pl.pallas_call(
         functools.partial(overlap_kernel, count),
         out_shape=jax.ShapeDtypeStruct((count, width, width), jnp.float32),
-        grid=(cells,),
+        grid=(cells // group,),
         in_specs=[block] * (count + 1),
         out_specs=pl.BlockSpec((count, width, width), lambda g: (0, 0, 0)),
         compiler_params=pltpu.CompilerParams(vmem_limit_bytes=32 * 2**20),
@@ -89,11 +94,210 @@
     )(*nows, folded)
 
 
+def flip(index, mask, size):
+    bit = 1
+    while bit < size:
+        if mask & bit:
+            index = index + bit * (1 - 2 * ((index // bit) % 2))
+        bit *= 2
+    return index
+
+
+def peer(dom, band):
+    return {"dom": dom, "band": band}
+
+
+def total_kernel(size, scale, part_ref, out_ref, inbox, piece, send_a, recv_a, send_b, recv_b):
+    me = lax.axis_index("dom")
+    band = lax.axis_index("band")
+    rows = part_ref.shape[0] // size
+    barrier = pltpu.get_barrier_semaphore()
+    for k in range(1, size):
+        pl.semaphore_signal(
+            barrier, inc=1, device_id=peer(flip(me, k, size), band), device_id_type=pl.DeviceIdType.MESH
+        )
+    pl.semaphore_wait(barrier, size - 1)
+
+    def chunk(at):
+        return pl.ds(pl.multiple_of(at * rows, rows), rows)
+
+    order = list(range(size - 1, 0, -1))
+    scatter = {}
+    for k in order:
+        other = flip(me, k, size)
+        scatter[k] = pltpu.make_async_remote_copy(
+            src_ref=part_ref.at[chunk(other)],
+            dst_ref=inbox.at[k],
+            send_sem=send_a.at[k],
+            recv_sem=recv_a.at[k],
+            device_id=peer(other, band),
+            device_id_type=pl.DeviceIdType.MESH,
+        )
+        scatter[k].start()
+    total = part_ref[chunk(me)]
+    for k in reversed(order):
+        scatter[k].wait_recv()
+        total = total + inbox[k]
+    piece[...] = (total * scale).astype(jnp.bfloat16)
+    spread = {}
+    for k in order:
+        spread[k] = pltpu.make_async_remote_copy(
+            src_ref=piece,
+            dst_ref=out_ref.at[chunk(me)],
+            send_sem=send_b.at[k],
+            recv_sem=recv_b.at[k],
+            device_id=peer(flip(me, k, size), band),
+            device_id_type=pl.DeviceIdType.MESH,
+        )
+        spread[k].start()
+    out_ref[chunk(me)] = piece[...]
+    for k in order:
+        scatter[k].wait_send()
+        spread[k].wait()
+
+
+def total_over_dom(part, scale):
+    size = lax.axis_size("dom")
+    rows, width = part.shape
+    return pl.pallas_call(
+        functools.partial(total_kernel, size, scale),
+        out_shape=jax.ShapeDtypeStruct(part.shape, jnp.bfloat16),
+        in_specs=[pl.BlockSpec(memory_space=pltpu.VMEM)],
+        out_specs=pl.BlockSpec(memory_space=pltpu.VMEM),
+        scratch_shapes=[
+            pltpu.VMEM((size, rows // size, width), jnp.float32),
+            pltpu.VMEM((rows // size, width), jnp.bfloat16),
+        ]
+        + [pltpu.SemaphoreType.DMA((size,))] * 4,
+        compiler_params=pltpu.CompilerParams(
+            collective_id=0, has_side_effects=True, vmem_limit_bytes=32 * 2**20
+        ),
+        name="total",
+    )(part)
+
+
+def exchange_kernel(size, bands, window, src_ref, out_ref, mid, send_a, recv_a, send_b, recv_b, local):
+    me = lax.axis_index("dom")
+    band = lax.axis_index("band")
+    cap = src_ref.shape[0] // size
+    sources = size // bands
+    barrier = pltpu.get_barrier_semaphore()
+    for k in range(1, size):
+        pl.semaphore_signal(
+            barrier, inc=1, device_id=peer(flip(me, k, size), band), device_id_type=pl.DeviceIdType.MESH
+        )
+    for k in range(1, bands):
+        pl.semaphore_signal(
+            barrier, inc=1, device_id=peer(me, flip(band, k, bands)), device_id_type=pl.DeviceIdType.MESH
+        )
+    pl.semaphore_wait(barrier, size + bands - 2)
+
+    def over_dom(k):
+        other = flip(me, k, size)
+        return pltpu.make_async_remote_copy(
+            src_ref=src_ref.at[pl.ds(other * cap, cap)],
+            dst_ref=mid.at[k],
+            send_sem=send_a.at[k],
+            recv_sem=recv_a.at[k],
+            device_id=peer(other, band),
+            device_id_type=pl.DeviceIdType.MESH,
+        )
+
+    def place(k):
+        source = flip(me, k, size)
+        block = mid.at[k] if k else src_ref.at[pl.ds(me * cap, cap)]
+        return block, source // sources, source % sources
+
+    def stay(k):
+        block, _, at = place(k)
+        return pltpu.make_async_copy(block, out_ref.at[band, pl.ds(at * cap, cap)], local.at[k])
+
+    def over_band(k):
+        block, target, at = place(k)
+        return pltpu.make_async_remote_copy(
+            src_ref=block,
+            dst_ref=out_ref.at[band, pl.ds(at * cap, cap)],
+            send_sem=send_b.at[k],
+            recv_sem=recv_b.at[band, at],
+            device_id=peer(me, target),
+            device_id_type=pl.DeviceIdType.MESH,
+        )
+
+    def pass_on(k):
+        _, target, _ = place(k)
+
+        @pl.when(target == band)
+        def _():
+            stay(k).start()
+
+        @pl.when(target != band)
+        def _():
+            over_band(k).start()
+
+    far = list(range(size // 2, size))
+    near = list(range(size // 2 - 1, 0, -1))
+    order = []
+    for at in range(len(far)):
+        order.append(far[at])
+        if at < len(near):
+            order.append(near[at])
+    for k in order[:window]:
+        over_dom(k).start()
+    pass_on(0)
+    for at, k in enumerate(order):
+        over_dom(k).wait_recv()
+        pass_on(k)
+        over_dom(k).wait_send()
+        if at + window < len(order):
+            over_dom(order[at + window]).start()
+    for k in range(size):
+        _, target, _ = place(k)
+
+        @pl.when(target == band)
+        def _():
+            stay(k).wait()
+
+        @pl.when(target != band)
+        def _():
+            over_band(k).wait_send()
+
+    for k in range(1, bands):
+        giver = flip(band, k, bands)
+        for at in range(sources):
+            pltpu.make_async_remote_copy(
+                src_ref=src_ref.at[pl.ds(at * cap, cap)],
+                dst_ref=out_ref.at[giver, pl.ds(at * cap, cap)],
+                send_sem=send_b.at[0],
+                recv_sem=recv_b.at[giver, at],
+                device_id=peer(me, giver),
+                device_id_type=pl.DeviceIdType.MESH,
+            ).wait_recv()
+
+
+def exchange(outgoing):
+    size, bands = lax.axis_size("dom"), lax.axis_size("band")
+    slots, width, nodes = outgoing.shape
+    cap, sources = slots // size, size // bands
+    return pl.pallas_call(
+        functools.partial(exchange_kernel, size, bands, 3),
+        out_shape=jax.ShapeDtypeStruct((bands, slots // bands, width, nodes), outgoing.dtype),
+        in_specs=[pl.BlockSpec(memory_space=pl.ANY)],
+        out_specs=pl.BlockSpec(memory_space=pl.ANY),
+        scratch_shapes=[pltpu.VMEM((size, cap, width, nodes), outgoing.dtype)]
+        + [pltpu.SemaphoreType.DMA((size,))] * 3
+        + [pltpu.SemaphoreType.DMA((bands, sources)), pltpu.SemaphoreType.DMA((size,))],
+        compiler_params=pltpu.CompilerParams(
+            collective_id=1, has_side_effects=True, vmem_limit_bytes=32 * 2**20
+        ),
+        name="exchange",
+    )(outgoing)
+
+
 def correct_kernel(count, slot_ref, *refs):
     now_refs, prev_ref, mix_ref, out_ref = refs[:count], refs[count], refs[count + 1], refs[count + 2]
     total = prev_ref[0].astype(jnp.float32)
     for k in range(count):
-        total = total + mm(mix_ref[k], now_refs[k][0], TN)
+        total = total + mm(mix_ref[k], now_refs[k][0])
     out_ref[0] = total.astype(jnp.bfloat16)
 
 
@@ -178,15 +382,14 @@
     valid = jnp.sum(hit, axis=2).reshape(-1)
     slot_oct = jnp.sum(hit[..., None] * near_oct[:, None], axis=2).reshape(-1, 2)
 
-    nows = gather_band(orbitals_now)
     folded = fold(orbitals_prev, interp, my_octants)
+    nows, folded = gather_band(orbitals_now, folded)
     partial = overlap(nows, folded)
     scaling = 1.0 / math.sqrt(2.0 * states * owner_map.shape[0] * node_count)
-    mix = (lax.psum(partial, "dom") * scaling).astype(jnp.bfloat16)
+    mix = total_over_dom(partial.reshape(states, state_dev), scaling)
+    mix = jnp.swapaxes(mix.reshape(partial.shape), 1, 2)
     outgoing = correct(nows, orbitals_prev, mix, slot_index, dom_size * capacity)
-    received = lax.all_to_all(outgoing, "dom", split_axis=0, concat_axis=0, tiled=True)
-    rows = lax.all_to_all(received, "band", split_axis=0, concat_axis=0, tiled=True)
-    rows = rows.reshape(band_size, slot_count, state_dev, node_count)
+    rows = exchange(outgoing)
     return expand(rows, interp, valid, slot_oct)
 
 

time: 346 us -> 208 us (0.60)
  waiting for transfers between devices: 160 us -> 29.1 us
  Pallas kernels: 51.6 us -> 161 us
  blocking collectives: 93.3 us -> 0 us
  between operations: 13.5 us -> 0.14 us
  starting transfers between devices: 11 us -> 3.74 us
    pallas_call x0 -> x2, Pallas kernels: none -> 121 us  [the longest x1 108 us: exchange(): pl.pallas_call(functools.partial(exchange_kernel, size, bands, 3), out_sh...]
    all_to_all x1 -> x0, blocking collectives: 93.3 us -> none  [per_device(): lax.all_to_all(outgoing, 'dom', split_axis=0, concat_axis=0, tiled=True)]
    psum x1 -> x0, waiting for transfers between devices: 68.5 us -> none  [per_device(): mix = (lax.psum(partial, 'dom') * scaling).astype(jnp.bfloat16)]
    all_to_all x1 -> x0, waiting for transfers between devices: 46.7 us -> none  [per_device(): lax.all_to_all(received, 'band', split_axis=0, concat_axis=0, tiled=True)]
    ppermute x3, waiting for transfers between devices: 44.6 us -> 29.1 us  [gather_band(): have[off ^ bit] = lax.ppermute(have[off], 'band', perm)]
    all_to_all x1 -> x0, starting transfers between devices: 7.28 us -> none  [per_device(): lax.all_to_all(received, 'band', split_axis=0, concat_axis=0, tiled=True)]
    pallas_call x1, Pallas kernels: 11.9 us -> 5 us  [overlap(): pl.pallas_call(functools.partial(overlap_kernel, count), out_shape=jax.Sh...]
    pallas_call x1, Pallas kernels: 15.6 us -> 10.9 us  [expand(): pl.pallas_call(expand_kernel, out_shape=jax.ShapeDtypeStruct((2 * slots,...]
  transfers between devices with their start and end apart: 5 -> 3, of which waited for: 3 -> 2; matrix products, arithmetic and copies ran while one was open for 1% -> 1% of each run, Pallas kernels for 4% -> 6%
where the time goes in v2:
time: 208 us; the launch traced here: 204 us
  Pallas kernels  161 us (77%)
  waiting for transfers between devices  29.1 us (14%)
  local copies, waits for them, and re-layouts  9.73 us (5%)
  starting transfers between devices  3.74 us (2%)
    pallas_call x1, Pallas kernels, exchange(): pl.pallas_call(functools.partial(exchange_kernel, size, bands, 3), out_sh...  108 us
    ppermute x3, waiting for transfers between devices, gather_band(): have[off ^ bit] = lax.ppermute(have[off], 'band', perm)  29.1 us
    pallas_call x1, Pallas kernels, total_over_dom(): pl.pallas_call(functools.partial(total_kernel, size, scale), out_shape=ja...  13.3 us
    pallas_call x1, Pallas kernels, fold(): pl.pallas_call(fold_kernel, out_shape=jax.ShapeDtypeStruct(prev.shape, jn...  12.4 us
    pallas_call x1, Pallas kernels, correct(): pl.pallas_call(functools.partial(correct_kernel, count), out_shape=jax.Sh...  11.6 us
    pallas_call x1, Pallas kernels, expand(): pl.pallas_call(expand_kernel, out_shape=jax.ShapeDtypeStruct((2 * slots,...  10.9 us
    unnamed x17, local copies, waits for them, and re-layouts  8.37 us
    pallas_call x1, Pallas kernels, overlap(): pl.pallas_call(functools.partial(overlap_kernel, count), out_shape=jax.Sh...  5 us
  transfers between devices with their start and end apart: 3, of which 2 were waited for; matrix products, arithmetic and copies ran while one was open for 1% of the time, Pallas kernels for 6%

profile of v2, /device:TPU:19, one launch (start us, length us, event | category | flops | bytes accessed | tf_op | source)
XLA Modules:
  0.0 204.4 jit_solution(11854387555849838985)
XLA Ops:
  0.0 1.2 collective-permute-start.1
  1.2 1.0 collective-permute-start
  2.2 0.8 reshape.38
  3.0 0.1 reshape.39.oct_ref
  3.2 2.2 %copy-done.1 = bf16[8,512,512]{2,1,0:T(8,128)(2,1)S(1)} copy-done((bf16[8,512,512]{2,1,0:T(8,128)(2,1)S(1)}, bf16[8,512,512]{2,1,0:T(8,128)(2,1)}, u32[]{:S(2)}) %copy-start.1) | copy-done | bytes 4194328
  5.3 1.6 copy-done.3
  6.9 12.4 %fold.1.refs_4_ = bf16[16,128,512]{2,1,0:T(8,128)(2,1)S(1)} custom-call(s32[32]{0:T(128)S(1)} %reshape.39.oct_ref, bf16[16,128,512]{2,1,0:T(8,128)(2,1)S(1)} %copy-done.3, bf16[8,512,512]{2,1,0:T(8,128)(2,1)S(1)} %copy-done.1, bf16[8,512,512]{2,1,0:T(8,128)(2,1)S(1)} %copy-done.1), custom_call_target="tpu_custom_call" | custom-call | flops 4294967296 | bytes 20971520 | tf_op jit(solution)/shard_map/fold/pallas_call | solution.py:44
  19.4 1.3 copy-done.5
  20.7 26.1 %collective-permute-done.1.refs_2_ = bf16[16,128,512]{2,1,0:T(8,128)(2,1)} collective-permute-done((bf16[16,128,512]{2,1,0:T(8,128)(2,1)}, bf16[16,128,512]{2,1,0:T(8,128)(2,1)}, u32[]{:S(2)}, u32[]{:S(2)}) %collective-permute-start.1) | collective-permute-done | bytes 2097184 | tf_op jit(solution)/shard_map/ppermute | solution.py:25
  46.8 1.5 collective-permute-start.2
  48.5 0.3 convert_reduce_fusion
  48.8 0.2 fusion.1
  49.1 0.1 multiply_reduce_fusion
  49.3 0.1 copy.12
  49.4 0.1 reshape_reshape.3.oct_ref
  49.5 3.0 %collective-permute-done.2.refs_3_ = bf16[16,128,512]{2,1,0:T(8,128)(2,1)} collective-permute-done((bf16[16,128,512]{2,1,0:T(8,128)(2,1)}, bf16[16,128,512]{2,1,0:T(8,128)(2,1)}, u32[]{:S(2)}, u32[]{:S(2)}) %collective-permute-start.2) | collective-permute-done | bytes 2097184 | tf_op jit(solution)/shard_map/ppermute | solution.py:25
  52.5 1.6 copy-done.6
  54.1 5.0 %overlap.1 = f32[4,128,128]{2,1,0:T(8,128)S(1)} custom-call(bf16[16,128,512]{2,1,0:T(8,128)(2,1)S(1)} %copy-done, bf16[16,128,512]{2,1,0:T(8,128)(2,1)} %collective-permute-done.refs_1_, bf16[16,128,512]{2,1,0:T(8,128)(2,1)} %collective-permute-done.1.refs_2_, bf16[16,128,512]{2,1,0:T(8,128)(2,1)} %collective-permute-done.2.refs_3_, ...), custom_call_target="tpu_custom_call" | custom-call | tf_op jit(solution)/shard_map/overlap/pallas_call | solution.py:86
  59.1 13.3 %total.1 = bf16[512,128]{1,0:T(8,128)(2,1)S(1)} custom-call(f32[512,128]{1,0:T(8,128)S(1)} %bitcast.7), custom_call_target="tpu_custom_call" | custom-call | tf_op jit(solution)/shard_map/total/pallas_call | solution.py:162
  72.4 0.1 copy.14
  72.5 1.6 copy-done.4
  74.1 11.6 %correct.1.src_ref = bf16[32,128,512]{2,1,0:T(8,128)(2,1)S(1)} custom-call(s32[16]{0:T(128)S(1)} %fusion.slot_ref, bf16[16,128,512]{2,1,0:T(8,128)(2,1)S(1)} %copy-done, bf16[16,128,512]{2,1,0:T(8,128)(2,1)} %collective-permute-done.refs_1_, bf16[16,128,512]{2,1,0:T(8,128)(2,1)} %collective-permute-done.1.refs_2_, ...), custom_call_target="tpu_custom_call" | custom-call | tf_op jit(solution)/shard_map/correct/pallas_call | solution.py:308
  85.7 107.7 %exchange.1.rows_ref = bf16[4,8,128,512]{3,2,1,0:T(8,128)(2,1)S(1)} custom-call(bf16[32,128,512]{2,1,0:T(8,128)(2,1)S(1)} %correct.1.src_ref), custom_call_target="tpu_custom_call" | custom-call | tf_op jit(solution)/shard_map/exchange/pallas_call | solution.py:281
  193.4 10.9 %expand.1 = bf16[16,512,512]{2,1,0:T(8,128)(2,1)} custom-call(s32[8]{0:T(128)S(1)} %reshape.37.valid_ref, s32[16]{0:T(128)S(1)} %reshape_reshape.3.oct_ref, bf16[4,8,128,512]{3,2,1,0:T(8,128)(2,1)S(1)} %exchange.1.rows_ref, bf16[8,512,512]{2,1,0:T(8,128)(2,1)S(1)} %copy-done.2), custom_call_target="tpu_custom_call" | custom-call | tf_op jit(solution)/shard_map/expand/pallas_call | solution.py:341
  (24 shorter events, 0.4 us)
Async XLA Ops:
  0.0 46.8 %collective-permute-start.1 = (bf16[16,128,512]{2,1,0:T(8,128)(2,1)}, bf16[16,128,512]{2,1,0:T(8,128)(2,1)}, u32[]{:S(2)}, u32[]{:S(2)}) collective-permute-start(bf16[16,128,512]{2,1,0:T(8,128)(2,1)} %refs_0_.3), channel_id=1, source_target_pairs={{0,2},{1,3},{2,0},{3,1},{4,6},{5,7},{6,4},{7,5},{8,10},{9,11},{10,... | collective-permute-start | bytes 6291464 | tf_op jit(solution)/shard_map/ppermute | solution.py:25
  1.2 48.2 %collective-permute-start = (bf16[16,128,512]{2,1,0:T(8,128)(2,1)}, bf16[16,128,512]{2,1,0:T(8,128)(2,1)}, u32[]{:S(2)}, u32[]{:S(2)}) collective-permute-start(bf16[16,128,512]{2,1,0:T(8,128)(2,1)} %refs_0_.3), channel_id=1, source_target_pairs={{0,1},{1,0},{2,3},{3,2},{4,5},{5,4},{6,7},{7,6},{8,9},{9,8},{10,11... | collective-permute-start | bytes 6291464 | tf_op jit(solution)/shard_map/ppermute | solution.py:25
  3.1 2.2 %copy-start.1 = (bf16[8,512,512]{2,1,0:T(8,128)(2,1)S(1)}, bf16[8,512,512]{2,1,0:T(8,128)(2,1)}, u32[]{:S(2)}) copy-start(bf16[8,512,512]{2,1,0:T(8,128)(2,1)} %interp_ref.1) | copy-start | bytes 12582916
  5.3 1.6 copy-start.3
  6.9 41.4 %copy-start.7 = (s32[128]{0:T(128)S(1)}, s32[128]{0:T(128)}, u32[]{:S(2)}) copy-start(s32[128]{0:T(128)} %param.8) | copy-start | bytes 1540
  6.9 45.6 %copy-start = (bf16[16,128,512]{2,1,0:T(8,128)(2,1)S(1)}, bf16[16,128,512]{2,1,0:T(8,128)(2,1)}, u32[]{:S(2)}) copy-start(bf16[16,128,512]{2,1,0:T(8,128)(2,1)} %refs_0_.3) | copy-start | bytes 6291460
  19.4 1.3 copy-start.5
  46.8 5.7 %collective-permute-start.2 = (bf16[16,128,512]{2,1,0:T(8,128)(2,1)}, bf16[16,128,512]{2,1,0:T(8,128)(2,1)}, u32[]{:S(2)}, u32[]{:S(2)}) collective-permute-start(bf16[16,128,512]{2,1,0:T(8,128)(2,1)} %collective-permute-done.1.refs_2_), channel_id=1, source_target_pairs={{0,1},{1,0},{2,3},{3,2},{4,5},{5,4},{6,7},{7,6},{8,9},{9,8},{10,11... | collective-permute-start | bytes 6291464 | tf_op jit(solution)/shard_map/ppermute | solution.py:25
  52.5 1.6 copy-start.6
  72.5 1.6 copy-start.4
  85.7 107.7 %copy-start.2 = (bf16[8,512,512]{2,1,0:T(8,128)(2,1)S(1)}, bf16[8,512,512]{2,1,0:T(8,128)(2,1)}, u32[]{:S(2)}) copy-start(bf16[8,512,512]{2,1,0:T(8,128)(2,1)} %interp_ref.1) | copy-start | bytes 12582916
